TPU v7x, 32 devices: a whole 2x2x4 slice. The times are simulated.
32 devices in a mesh: user: 8 (over z, y), item: 4 (over x, core).
Axes of the slice: x: 2, y: 2, z: 4, core: 2. Of those that a mesh axis runs over, the one named last changes fastest.
Arguments:
- item_features: bfloat16 [2048, 2048], P(('item', 'user')), may hold values from -6 to 6
- layer_one: bfloat16 [2048, 1024], replicated, may hold values from -0.125 to 0.125
- layer_two: bfloat16 [1024, 512], replicated, may hold values from -0.1875 to 0.1875
- log_weight: float32 [2048], P(('item', 'user')), may hold values from 0 to 4.9
- user_vectors: bfloat16 [4096, 512], P('user'), may hold values from -360 to 360
- positive_index: int32 [4096], P('user'), may hold values from 0 to 2047
Outputs:
- row_loss: float32 [4096], P('user')
- col_lse: float32 [2048], P(('item', 'user'))
All inputs are finite; a program needn't handle non-finite values.
Results may differ from a plain program's by a relative error of at most 0.007.
Values may be sent and summed in bfloat16 or wider, within the bound.
A program may use at most 64 MiB of HBM per device.

v0:
```python
import math

import jax
import jax.numpy as jnp
from jax import lax
from jax.sharding import PartitionSpec as P


def merged(array, axis, combine):
    everything = jax.tree.map(lambda part: lax.all_gather(part, axis), array)
    initial = jax.tree.map(lambda part: part[0], everything)

    def step(k, so_far):
        return combine(so_far, jax.tree.map(lambda part: part[k], everything))

    return lax.fori_loop(1, lax.axis_size(axis), step, initial)


def combined_all(array, axis, combine):
    everything = jax.tree.map(
        lambda part, kind: lax.all_gather(part.astype(kind), axis),
        array,
        (jnp.bfloat16, jnp.bfloat16),
    )

    def take(k):
        return jax.tree.map(lambda part, own: part[k].astype(own.dtype), everything, array)

    return lax.fori_loop(
        1, lax.axis_size(axis), lambda k, so_far: combine(so_far, take(k)), take(0)
    )


def join_pair(first, second):
    top = jnp.maximum(first[0], second[0])
    total = first[1] * jnp.exp(first[0] - top) + second[1] * jnp.exp(second[0] - top)
    return (top, total)


def on_device(item_features, layer_one, layer_two, log_weight, user_vectors, positive_index):
    hidden = jax.nn.relu(
        jnp.dot(item_features, layer_one, preferred_element_type=jnp.float32)
    ).astype(jnp.bfloat16)
    embedded = jnp.dot(hidden, layer_two, preferred_element_type=jnp.float32).astype(jnp.bfloat16)
    users = user_vectors.shape[0]
    per_device = item_features.shape[0]
    inverse_temp = 4.0 / math.sqrt(user_vectors.shape[1])
    user_count = lax.axis_size("user")
    group = per_device * user_count
    group_start = lax.axis_index("item") * group
    row_max = jnp.full((users,), -1e30, jnp.float32)
    row_sum = jnp.zeros((users,), jnp.float32)
    row_positive = jnp.zeros((users,), jnp.float32)
    piece_vectors = lax.all_gather(embedded, "user", axis=0, tiled=True)
    piece_weight = lax.all_gather(
        log_weight.astype(jnp.bfloat16), "user", axis=0, tiled=True
    ).astype(jnp.float32)
    count = piece_vectors.shape[0]
    scores = (
        lax.dot_general(
            user_vectors,
            piece_vectors,
            (((1,), (1,)), ((), ())),
            preferred_element_type=jnp.float32,
        )
        * inverse_temp
    )
    top_col = jnp.max(scores, axis=0)
    sum_col = jnp.sum(jnp.exp(scores - top_col[None, :]), axis=0)
    col_max = top_col
    col_sum = sum_col
    logits = scores + piece_weight[None, :]
    new_max = jnp.maximum(row_max, jnp.max(logits, axis=1))
    row_sum = row_sum * jnp.exp(row_max - new_max) + jnp.sum(
        jnp.exp(logits - new_max[:, None]), axis=1
    )
    columns = group_start + lax.iota(jnp.int32, count)
    hits = positive_index[:, None] == columns[None, :]
    row_positive = row_positive + jnp.sum(jnp.where(hits, logits, 0.0), axis=1)
    row_max, row_sum, row_positive, col_max, col_sum = (
        new_max,
        row_sum,
        row_positive,
        col_max,
        col_sum,
    )
    top, total = merged((row_max, row_sum), "item", join_pair)
    positive = lax.psum(row_positive, "item")
    row_loss = top + jnp.log(total) - positive
    all_max, all_sum = combined_all((col_max, col_sum), "user", join_pair)
    every_lse = all_max + jnp.log(all_sum)
    col_lse = lax.dynamic_slice_in_dim(
        every_lse, lax.axis_index("user") * per_device, per_device, 0
    )
    return (row_loss, col_lse)


def solution(mesh):
    placed = (P(("item", "user"), None), P(), P(), P(("item", "user")), P("user", None), P("user"))
    return jax.shard_map(
        on_device,
        mesh=mesh,
        in_specs=placed,
        out_specs=(P("user"), P(("item", "user"))),
        check_vma=False,
    )
```

profile of v0, /device:TPU:0, one launch (start us, length us, event | category | flops | bytes accessed | tf_op | source)
XLA Modules:
  0.0 132.6 jit_solution(6278166053230662933)
XLA Ops:
  0.6 0.0 copy-start
  0.6 0.0 copy-start.4
  0.7 0.0 copy-start.1
  0.7 0.0 copy-start.3
  0.7 1.4 %copy-done = bf16[1024,512]{1,0:T(8,128)(2,1)S(1)} copy-done((bf16[1024,512]{1,0:T(8,128)(2,1)S(1)}, bf16[1024,512]{1,0:T(8,128)(2,1)}, u32[]{:S(2)}) %copy-start) | copy-done | bytes 1048600
  2.0 0.0 copy-start.2
  2.0 3.3 %fusion.2 = bf16[64,512]{1,0:T(8,128)(2,1)S(1)} fusion(bf16[1024,512]{1,0:T(8,128)(2,1)S(1)} %copy-done, bf16[64,2048]{1,0:T(8,128)(2,1)} %param.10, bf16[2048,1024]{1,0:T(8,128)(2,1)} %param.11), kind=kOutput, calls=%fused_computation.10 | convolution fusion | flops 335708160 | bytes 5570560 | tf_op jit(solution)/shard_map/dot_general | solution.py:44
  5.4 33.0 %all_gather.22 = bf16[512,512]{1,0:T(8,128)(2,1)S(1)} all-gather(bf16[64,512]{1,0:T(8,128)(2,1)S(1)} %fusion.2), channel_id=1, replica_groups=mesh['user'=8,'item'=4] {'user'}, dimensions={0}, use_global_device_ids=true | all-gather | bytes 589824 | tf_op jit(solution)/shard_map/all_gather | solution.py:54
  38.4 0.0 copy-done.1
  38.4 0.6 fusion.8
  38.9 0.0 copy-done.3
  38.9 0.0 copy-done.4
  39.0 0.6 dynamic-slice
  40.2 0.2 dynamic-update-slice
  40.5 21.5 %all-reduce = bf16[512]{0:T(512)(128)(2,1)S(1)} all-reduce(bf16[512]{0:T(512)(128)(2,1)S(1)} %dynamic-update-slice), channel_id=1, replica_groups=mesh['user'=8,'item'=4] {'user'}, use_global_device_ids=true, to_apply=%add | all-reduce | flops 512 | bytes 2048
  62.0 0.4 exponential_reduce_fusion
  62.4 0.0 copy-done.2
  62.4 0.4 fusion.4
  62.8 5.7 %psum.7 = f32[512]{0:T(512)S(1)} all-reduce(f32[512]{0:T(512)S(1)} %get-tuple-element.273), channel_id=1, replica_groups=mesh['user'=8,'item'=4] {'item'}, use_global_device_ids=true, to_apply=%region_5.6 | all-reduce | flops 512 | bytes 4096 | tf_op jit(solution)/shard_map/psum | solution.py:88
  68.4 5.2 %all-gather.3 = f32[4,1,512]{2,1,0:T(1,128)S(1)} all-gather(f32[1,1,512]{2,1,0:T(1,128)S(1)} %bitcast.57), channel_id=2, replica_groups=mesh['user'=8,'item'=4] {'item'}, dimensions={0}, use_global_device_ids=true | all-gather | bytes 10240 | tf_op jit(solution)/shard_map/all_gather | solution.py:10
  73.6 5.2 %all-gather.4 = f32[4,1,512]{2,1,0:T(1,128)S(1)} all-gather(f32[1,1,512]{2,1,0:T(1,128)S(1)} %bitcast.58), channel_id=1, replica_groups=mesh['user'=8,'item'=4] {'item'}, dimensions={0}, use_global_device_ids=true | all-gather | bytes 10240 | tf_op jit(solution)/shard_map/all_gather | solution.py:10
  78.8 0.2 while.34
  78.9 0.6 add_subtract_fusion
  79.5 26.0 %all-gather.5 = bf16[8,1,512]{2,1,0:T(2,128)(2,1)S(1)} all-gather(bf16[1,1,512]{2,1,0:T(2,128)(2,1)S(1)} %reshape.95), channel_id=3, replica_groups=mesh['user'=8,'item'=4] {'user'}, dimensions={0}, use_global_device_ids=true | all-gather | bytes 9216 | tf_op jit(solution)/shard_map/all_gather | solution.py:21
  105.5 26.0 %all-gather.6 = bf16[8,1,512]{2,1,0:T(2,128)(2,1)S(1)} all-gather(bf16[1,1,512]{2,1,0:T(2,128)(2,1)S(1)} %reshape.97), channel_id=4, replica_groups=mesh['user'=8,'item'=4] {'user'}, dimensions={0}, use_global_device_ids=true | all-gather | bytes 9216 | tf_op jit(solution)/shard_map/all_gather | solution.py:21
  131.6 0.4 while.35
  132.0 0.6 dynamic_slice.43
  (38 shorter events, 0.4 us)
Async XLA Ops:
  0.6 1.4 %copy-start = (bf16[1024,512]{1,0:T(8,128)(2,1)S(1)}, bf16[1024,512]{1,0:T(8,128)(2,1)}, u32[]{:S(2)}) copy-start(bf16[1024,512]{1,0:T(8,128)(2,1)} %param.12) | copy-start | bytes 3145732
  0.6 38.3 %copy-start.4 = (u32[32]{0:T(128)S(1)}, u32[32]{0:T(128)}, u32[]{:S(2)}) copy-start(u32[32]{0:T(128)} %constant.99) | copy-start | bytes 388
  0.7 37.7 %copy-start.1 = (bf16[512,512]{1,0:T(8,128)(2,1)S(1)}, bf16[512,512]{1,0:T(8,128)(2,1)}, u32[]{:S(2)}) copy-start(bf16[512,512]{1,0:T(8,128)(2,1)} %param.14) | copy-start | bytes 1572868
  0.7 38.3 %copy-start.3 = (f32[64]{0:T(128)S(1)}, f32[64]{0:T(128)}, u32[]{:S(2)}) copy-start(f32[64]{0:T(128)} %param.13) | copy-start | bytes 772
  2.0 60.4 %copy-start.2 = (s32[512]{0:T(512)S(1)}, s32[512]{0:T(512)}, u32[]{:S(2)}) copy-start(s32[512]{0:T(512)} %param.15) | copy-start | bytes 6148
where the time goes:
time: 133 us
  blocking collectives  122 us (92%)
  matrix products  3.87 us (3%)
  local copies, waits for them, and re-layouts  2.86 us (2%)
  other arithmetic  1.64 us (1%)
  between operations  1.44 us (1%)
    all_gather x2, blocking collectives, combined_all(): lax.all_gather(part.astype(kind), axis)  52 us
    all_gather x1, blocking collectives, on_device(): piece_vectors = lax.all_gather(embedded, 'user', axis=0, tiled=True)  33 us
    unnamed x1, blocking collectives  21.5 us
    all_gather x2, blocking collectives, merged(): everything = jax.tree.map(lambda part: lax.all_gather(part, axis), array)  10.3 us
    psum x1, blocking collectives, on_device(): positive = lax.psum(row_positive, 'item')  5.67 us
    dot_general x1, matrix products, on_device(): jnp.dot(hidden, layer_two, preferred_element_type=jnp.float32)  3.31 us

commit v1 on v0

v1 whole, which is shorter than its diff:
```python
import functools
import math

import jax
import jax.numpy as jnp
from jax import lax
from jax.experimental import pallas as pl
from jax.experimental.pallas import tpu as pltpu
from jax.sharding import PartitionSpec as P

MESH = pl.DeviceIdType.MESH
CHUNKS = 4


def kernel(n_user, n_item, n_y, x_hbm, w1_hbm, w2_hbm, lw_ref, uv_hbm, pos_ref, row_ref, col_ref,
           xv, w1v, w2v, uvv, hv, emb, lwg, col_send, col_recv, row_send, row_recv,
           in_sem, w1_sem, lw_ssem, lw_rsem, z_ssem, y_ssem, emb_rsem, col_ssem, col_rsem, row_ssem, row_rsem):
    n_z = n_user // n_y
    u = lax.axis_index("user")
    i = lax.axis_index("item")
    z, y = u // n_y, u % n_y
    per = xv.shape[0]
    users = uvv.shape[0]
    inverse_temp = 4.0 / math.sqrt(uvv.shape[1])
    wide = hv.shape[1] // CHUNKS

    cx = pltpu.make_async_copy(x_hbm, xv, in_sem.at[0])
    cx.start()
    c1 = []
    for c in range(CHUNKS):
        cols = pl.ds(c * wide, wide)
        c1.append(pltpu.make_async_copy(w1_hbm.at[:, cols], w1v.at[:, cols], w1_sem.at[c]))
        c1[-1].start()
    c2 = pltpu.make_async_copy(w2_hbm, w2v, in_sem.at[1])
    c2.start()
    cu = pltpu.make_async_copy(uv_hbm, uvv, in_sem.at[2])
    cu.start()

    def user_at(d):
        return lax.rem(u + d, n_user)

    def item_at(d):
        return lax.rem(i + d, n_item)

    barrier = pltpu.get_barrier_semaphore()
    for d in range(1, n_user):
        pl.semaphore_signal(barrier, inc=1, device_id={"user": user_at(d)}, device_id_type=MESH)
    for d in range(1, n_item):
        pl.semaphore_signal(barrier, inc=1, device_id={"item": item_at(d)}, device_id_type=MESH)

    def to_user(src, dst, ssem, rsem, t):
        return pltpu.make_async_remote_copy(
            src_ref=src, dst_ref=dst, send_sem=ssem, recv_sem=rsem,
            device_id={"user": t}, device_id_type=MESH)

    def to_item(src, dst, ssem, rsem, t):
        return pltpu.make_async_remote_copy(
            src_ref=src, dst_ref=dst, send_sem=ssem, recv_sem=rsem,
            device_id={"item": t}, device_id_type=MESH)

    lwg[u] = jnp.zeros((8, 128), jnp.float32)
    lwg[u, 0:1, 0:per] = lw_ref[...]

    cx.wait()
    xs = xv[...]
    for c in range(CHUNKS):
        c1[c].wait()
        cols = slice(c * wide, (c + 1) * wide)
        part = jnp.dot(xs, w1v[:, cols], preferred_element_type=jnp.float32)
        hv[:, cols] = jnp.maximum(part, 0.0).astype(jnp.bfloat16)
        if c == CHUNKS - 2:
            pl.semaphore_wait(barrier, n_user + n_item - 2)
            for d in range(1, n_user):
                to_user(lwg.at[u], lwg.at[u], lw_ssem.at[d], lw_rsem.at[u], user_at(d)).start()
    c2.wait()
    emb[u] = jnp.dot(hv[...], w2v[...], preferred_element_type=jnp.float32).astype(jnp.bfloat16)

    def z_piece(d):
        return lax.rem(z + n_z - d, n_z) * n_y + y

    def y_piece(d, e):
        return lax.rem(z + n_z - d, n_z) * n_y + lax.rem(y + n_y - e, n_y)

    def forward(p, d):
        for e in range(1, n_y):
            t = z * n_y + lax.rem(y + e, n_y)
            to_user(emb.at[p], emb.at[p], y_ssem.at[d, e], emb_rsem.at[p], t).start()

    def arrive(p):
        to_user(emb.at[p], emb.at[p], z_ssem.at[0], emb_rsem.at[p], u).wait_recv()

    forward(u, 0)
    for d in range(1, n_z):
        t = lax.rem(z + d, n_z) * n_y + y
        to_user(emb.at[u], emb.at[u], z_ssem.at[d], emb_rsem.at[u], t).start()

    cu.wait()
    for d in range(1, n_user):
        p = user_at(d)
        to_user(lwg.at[p], lwg.at[p], lw_ssem.at[0], lw_rsem.at[p], u).wait_recv()

    eye = (lax.broadcasted_iota(jnp.int32, (per, 128), 0)
           == lax.broadcasted_iota(jnp.int32, (per, 128), 1))
    item_of = lax.broadcasted_iota(jnp.int32, (per, users), 0)
    group_start = i * n_user * per

    def piece(p, own, carry):
        row_max, row_sum, row_pos = carry
        scores = lax.dot_general(emb[p], uvv[...], (((1,), (1,)), ((), ())),
                                 preferred_element_type=jnp.float32) * inverse_temp
        top = jnp.max(scores, axis=1, keepdims=True)
        lse = top + jnp.log(jnp.sum(jnp.exp(scores - top), axis=1, keepdims=True))
        flat = jnp.sum(jnp.where(eye, lse, 0.0), axis=0, keepdims=True)
        tile = jnp.broadcast_to(flat, (8, 128))
        if own:
            col_recv[u] = tile
        else:
            col_send[p] = tile
            to_user(col_send.at[p], col_recv.at[u], col_ssem.at[p], col_rsem.at[u], p).start()
        weight = jnp.sum(jnp.where(eye, lwg[p, 0:1, :], 0.0), axis=1, keepdims=True)
        logits = scores + weight
        new_max = jnp.maximum(row_max, jnp.max(logits, axis=0, keepdims=True))
        row_sum = row_sum * jnp.exp(row_max - new_max) + jnp.sum(
            jnp.exp(logits - new_max), axis=0, keepdims=True)
        hits = pos_ref[...] == group_start + p * per + item_of
        row_pos = row_pos + jnp.sum(jnp.where(hits, logits, 0.0), axis=0, keepdims=True)
        return new_max, row_sum, row_pos

    carry = (jnp.full((1, users), -1e30, jnp.float32), jnp.zeros((1, users), jnp.float32),
             jnp.zeros((1, users), jnp.float32))
    carry = piece(u, True, carry)

    def y_step(d, carry):
        for e in range(1, n_y):
            p = y_piece(d, e)
            arrive(p)
            carry = piece(p, False, carry)
        return carry

    def step(d, carry):
        p = z_piece(d)
        arrive(p)
        forward(p, d)
        carry = piece(p, False, carry)
        return y_step(d - 1, carry)

    if n_user <= 8:
        for d in range(1, n_z):
            carry = step(d, carry)
    else:
        carry = lax.fori_loop(1, n_z, step, carry)
    carry = y_step(n_z - 1, carry)

    row_max, row_sum, row_pos = carry
    row_lse = row_max + jnp.log(row_sum)
    first = lax.broadcasted_iota(jnp.int32, (8, users), 0) == 0
    stats = jnp.where(first, row_lse, row_pos)
    row_send[...] = stats
    for d in range(1, n_item):
        to_item(row_send, row_recv.at[i], row_ssem.at[d], row_rsem.at[i], item_at(d)).start()
    row_recv[i] = stats

    for d in range(1, n_item):
        q = item_at(d)
        to_item(row_send, row_recv.at[q], row_ssem.at[0], row_rsem.at[q], i).wait_recv()
    lse_all = row_recv[:, 0, :]
    top = jnp.max(lse_all, axis=0, keepdims=True)
    total = top + jnp.log(jnp.sum(jnp.exp(lse_all - top), axis=0, keepdims=True))
    row_ref[...] = total - jnp.sum(row_recv[:, 1, :], axis=0, keepdims=True)

    for d in range(1, n_user):
        p = user_at(d)
        to_user(col_send.at[p], col_recv.at[p], col_ssem.at[0], col_rsem.at[p], u).wait_recv()
    lse_all = col_recv[:, 0, :]
    top = jnp.max(lse_all, axis=0, keepdims=True)
    total = top + jnp.log(jnp.sum(jnp.exp(lse_all - top), axis=0, keepdims=True))
    col_ref[...] = total[:, 0:per]

    for d in range(1, n_user):
        p = user_at(d)
        to_user(lwg.at[u], lwg.at[u], lw_ssem.at[d], lw_rsem.at[u], p).wait_send()
        to_user(col_send.at[p], col_recv.at[u], col_ssem.at[p], col_rsem.at[u], p).wait_send()
    for d in range(1, n_item):
        to_item(row_send, row_recv.at[i], row_ssem.at[d], row_rsem.at[i], item_at(d)).wait_send()
    for d in range(n_z):
        if d > 0:
            to_user(emb.at[u], emb.at[u], z_ssem.at[d], emb_rsem.at[u], u).wait_send()
        for e in range(1, n_y):
            to_user(emb.at[u], emb.at[u], y_ssem.at[d, e], emb_rsem.at[u], u).wait_send()


def on_device(n_user, n_item, n_y, item_features, layer_one, layer_two, log_weight, user_vectors,
              positive_index):
    per, d_in = item_features.shape
    d_hid, d_emb = layer_two.shape
    users = user_vectors.shape[0]
    anywhere = pl.BlockSpec(memory_space=pl.ANY)
    vmem = pl.BlockSpec(memory_space=pltpu.VMEM)
    dma = pltpu.SemaphoreType.DMA
    row, col = pl.pallas_call(
        functools.partial(kernel, n_user, n_item, n_y),
        out_shape=(jax.ShapeDtypeStruct((1, users), jnp.float32),
                   jax.ShapeDtypeStruct((1, per), jnp.float32)),
        in_specs=[anywhere, anywhere, anywhere, vmem, anywhere, vmem],
        out_specs=(vmem, vmem),
        scratch_shapes=[
            pltpu.VMEM((per, d_in), jnp.bfloat16),
            pltpu.VMEM((d_in, d_hid), jnp.bfloat16),
            pltpu.VMEM((d_hid, d_emb), jnp.bfloat16),
            pltpu.VMEM((users, d_emb), jnp.bfloat16),
            pltpu.VMEM((per, d_hid), jnp.bfloat16),
            pltpu.VMEM((n_user, per, d_emb), jnp.bfloat16),
            pltpu.VMEM((n_user, 8, 128), jnp.float32),
            pltpu.VMEM((n_user, 8, 128), jnp.float32),
            pltpu.VMEM((n_user, 8, 128), jnp.float32),
            pltpu.VMEM((8, users), jnp.float32),
            pltpu.VMEM((n_item, 8, users), jnp.float32),
            dma((3,)),
            dma((CHUNKS,)),
            dma((n_user,)),
            dma((n_user,)),
            dma((n_user // n_y,)),
            dma((n_user // n_y, n_y)),
            dma((n_user,)),
            dma((n_user,)),
            dma((n_user,)),
            dma((n_item,)),
            dma((n_item,)),
        ],
        compiler_params=pltpu.CompilerParams(
            collective_id=0, has_side_effects=True, vmem_limit_bytes=40 * 1024 * 1024),
    )(item_features, layer_one, layer_two, log_weight.reshape(1, per), user_vectors,
      positive_index.reshape(1, users))
    return row.reshape(users), col.reshape(per)


def solution(mesh):
    n_user, n_item = mesh.shape["user"], mesh.shape["item"]
    n_y = 1
    while n_user % (2 * n_y) == 0 and 8 * n_y * n_y <= n_user:
        n_y *= 2
    placed = (P(("item", "user"), None), P(), P(), P(("item", "user")), P("user", None), P("user"))
    return jax.shard_map(
        functools.partial(on_device, n_user, n_item, n_y),
        mesh=mesh,
        in_specs=placed,
        out_specs=(P("user"), P(("item", "user"))),
        check_vma=False,
    )
```

time: 133 us -> 33.5 us (0.25)
  blocking collectives: 122 us -> 0 us
  Pallas kernels: 0 us -> 24.7 us
  local copies, waits for them, and re-layouts: 2.86 us -> 7.82 us
  matrix products: 3.87 us -> 0 us
  other arithmetic: 1.64 us -> 0 us
    all_gather x5 -> x0, blocking collectives: 95.3 us -> none  [the longest x2 52 us: combined_all(): lax.all_gather(part.astype(kind), axis)]
    pallas_call x0 -> x1, Pallas kernels: none -> 24.7 us  [on_device(): pl.pallas_call(functools.partial(kernel, n_user, n_item, n_y), out_shape=...]
    unnamed x1 -> x0, blocking collectives: 21.5 us -> none
    psum x1 -> x0, blocking collectives: 5.67 us -> none  [on_device(): positive = lax.psum(row_positive, 'item')]
    unnamed x19 -> x14, local copies, waits for them, and re-layouts: 2.24 us -> 7.82 us
    dot_general x2 -> x0, matrix products: 3.87 us -> none  [the longest x1 3.31 us: on_device(): jnp.dot(hidden, layer_two, preferred_element_type=jnp.float32)]
where the time goes in v1:
time: 33.5 us; the launch traced here: 33.2 us
  Pallas kernels  24.7 us (74%)
  local copies, waits for them, and re-layouts  7.82 us (23%)
  between operations  0.65 us (2%)
    pallas_call x1, Pallas kernels, on_device(): pl.pallas_call(functools.partial(kernel, n_user, n_item, n_y), out_shape=...  24.7 us
    unnamed x14, local copies, waits for them, and re-layouts  7.82 us

profile of v1, /device:TPU:0, one launch (start us, length us, event | category | flops | bytes accessed | tf_op | source)
XLA Modules:
  0.0 33.2 jit_solution(14541155708699569587)
XLA Ops:
  0.6 0.0 copy-start
  0.6 2.2 %copy-done = bf16[2048,1024]{1,0:T(8,128)(2,1)S(1)} copy-done((bf16[2048,1024]{1,0:T(8,128)(2,1)S(1)}, bf16[2048,1024]{1,0:T(8,128)(2,1)}, u32[]{:S(2)}) %copy-start) | copy-done | bytes 4194328
  2.8 0.0 copy-start.1
  2.8 1.2 %copy-done.1 = bf16[1024,512]{1,0:T(8,128)(2,1)S(1)} copy-done((bf16[1024,512]{1,0:T(8,128)(2,1)S(1)}, bf16[1024,512]{1,0:T(8,128)(2,1)}, u32[]{:S(2)}) %copy-start.1) | copy-done | bytes 1048600
  4.0 0.0 copy-start.2
  4.0 1.0 %copy-done.2 = bf16[512,512]{1,0:T(8,128)(2,1)S(1)} copy-done((bf16[512,512]{1,0:T(8,128)(2,1)S(1)}, bf16[512,512]{1,0:T(8,128)(2,1)}, u32[]{:S(2)}) %copy-start.2) | copy-done | bytes 524312
  5.1 0.0 copy-start.3
  5.1 0.9 %copy-done.3 = bf16[64,2048]{1,0:T(8,128)(2,1)S(1)} copy-done((bf16[64,2048]{1,0:T(8,128)(2,1)S(1)}, bf16[64,2048]{1,0:T(8,128)(2,1)}, u32[]{:S(2)}) %copy-start.3) | copy-done | bytes 262168
  6.0 0.0 copy-start.4
  6.0 0.7 %copy-done.4 = s32[512]{0:T(512)S(1)} copy-done((s32[512]{0:T(512)S(1)}, s32[512]{0:T(512)}, u32[]{:S(2)}) %copy-start.4) | copy-done | bytes 2072
  6.7 0.0 copy-start.5
  6.7 0.7 %copy-done.5 = f32[64]{0:T(128)S(1)} copy-done((f32[64]{0:T(128)S(1)}, f32[64]{0:T(128)}, u32[]{:S(2)}) %copy-start.5) | copy-done | bytes 280
  7.4 24.7 %shard_map.77 = (f32[1,512]{1,0:T(1,128)S(1)}, f32[1,64]{1,0:T(1,128)S(1)}) custom-call(bf16[64,2048]{1,0:T(8,128)(2,1)S(1)} %copy-done.3, bf16[2048,1024]{1,0:T(8,128)(2,1)S(1)} %copy-done, bf16[1024,512]{1,0:T(8,128)(2,1)S(1)} %copy-done.1, f32[1,64]{1,0:T(1,128)S(1)} %bitcast.6, bf16[512,512]{1,0:T(8,128)(2,1)S(1)} %copy-done.2, s32[1,512]{1,0:T(1,128)S(1)} %bitcast.4), custom_call_target="tpu_custom_call" | custom-call | tf_op jit(solution)/shard_map/pallas_call | solution.py:200
  32.1 0.6 %copy.10 = f32[512]{0:T(512)} copy(f32[512]{0:T(512)S(1)} %bitcast.5) | data formatting | bytes 4096
  32.7 0.5 %copy.11 = f32[64]{0:T(128)} copy(f32[64]{0:T(128)S(1)} %bitcast.7) | data formatting | bytes 512
Async XLA Ops:
  0.6 2.2 %copy-start = (bf16[2048,1024]{1,0:T(8,128)(2,1)S(1)}, bf16[2048,1024]{1,0:T(8,128)(2,1)}, u32[]{:S(2)}) copy-start(bf16[2048,1024]{1,0:T(8,128)(2,1)} %w1_hbm.1) | copy-start | bytes 12582916
  2.8 1.2 %copy-start.1 = (bf16[1024,512]{1,0:T(8,128)(2,1)S(1)}, bf16[1024,512]{1,0:T(8,128)(2,1)}, u32[]{:S(2)}) copy-start(bf16[1024,512]{1,0:T(8,128)(2,1)} %w2_hbm.1) | copy-start | bytes 3145732
  4.0 1.0 %copy-start.2 = (bf16[512,512]{1,0:T(8,128)(2,1)S(1)}, bf16[512,512]{1,0:T(8,128)(2,1)}, u32[]{:S(2)}) copy-start(bf16[512,512]{1,0:T(8,128)(2,1)} %uv_hbm.1) | copy-start | bytes 1572868
  5.1 0.9 %copy-start.3 = (bf16[64,2048]{1,0:T(8,128)(2,1)S(1)}, bf16[64,2048]{1,0:T(8,128)(2,1)}, u32[]{:S(2)}) copy-start(bf16[64,2048]{1,0:T(8,128)(2,1)} %x_hbm.1) | copy-start | bytes 786436
  6.0 0.7 %copy-start.4 = (s32[512]{0:T(512)S(1)}, s32[512]{0:T(512)}, u32[]{:S(2)}) copy-start(s32[512]{0:T(512)} %param.11) | copy-start | bytes 6148
  6.7 0.7 %copy-start.5 = (f32[64]{0:T(128)S(1)}, f32[64]{0:T(128)}, u32[]{:S(2)}) copy-start(f32[64]{0:T(128)} %param.9) | copy-start | bytes 772

commit v2 on v1

--- a/solution.py
+++ b/solution.py
@@ -12,8 +12,8 @@
 CHUNKS = 4
 
 
-def kernel(n_user, n_item, n_y, x_hbm, w1_hbm, w2_hbm, lw_ref, uv_hbm, pos_ref, row_ref, col_ref,
-           xv, w1v, w2v, uvv, hv, emb, lwg, col_send, col_recv, row_send, row_recv,
+def kernel(n_user, n_item, n_y, x_hbm, w1_hbm, w2_hbm, lw_hbm, uv_hbm, pos_hbm, row_ref, col_ref,
+           xv, w1v, w2v, uvv, uvt, lw_ref, pos_ref, hv, emb, lwg, col_send, col_recv, row_send, row_recv,
            in_sem, w1_sem, lw_ssem, lw_rsem, z_ssem, y_ssem, emb_rsem, col_ssem, col_rsem, row_ssem, row_rsem):
     n_z = n_user // n_y
     u = lax.axis_index("user")
@@ -35,6 +35,10 @@
     c2.start()
     cu = pltpu.make_async_copy(uv_hbm, uvv, in_sem.at[2])
     cu.start()
+    cp = pltpu.make_async_copy(pos_hbm, pos_ref, in_sem.at[3])
+    cp.start()
+    cw = pltpu.make_async_copy(lw_hbm, lw_ref, in_sem.at[4])
+    cw.start()
 
     def user_at(d):
         return lax.rem(u + d, n_user)
@@ -59,6 +63,7 @@
             device_id={"item": t}, device_id_type=MESH)
 
     lwg[u] = jnp.zeros((8, 128), jnp.float32)
+    cw.wait()
     lwg[u, 0:1, 0:per] = lw_ref[...]
 
     cx.wait()
@@ -95,6 +100,9 @@
         to_user(emb.at[u], emb.at[u], z_ssem.at[d], emb_rsem.at[u], t).start()
 
     cu.wait()
+    cp.wait()
+    for r in range(0, users, 128):
+        uvt[:, r:r + 128] = uvv[r:r + 128, :].T
     for d in range(1, n_user):
         p = user_at(d)
         to_user(lwg.at[p], lwg.at[p], lw_ssem.at[0], lw_rsem.at[p], u).wait_recv()
@@ -106,8 +114,7 @@
 
     def piece(p, own, carry):
         row_max, row_sum, row_pos = carry
-        scores = lax.dot_general(emb[p], uvv[...], (((1,), (1,)), ((), ())),
-                                 preferred_element_type=jnp.float32) * inverse_temp
+        scores = jnp.dot(emb[p], uvt[...], preferred_element_type=jnp.float32) * inverse_temp
         top = jnp.max(scores, axis=1, keepdims=True)
         lse = top + jnp.log(jnp.sum(jnp.exp(scores - top), axis=1, keepdims=True))
         flat = jnp.sum(jnp.where(eye, lse, 0.0), axis=0, keepdims=True)
@@ -153,8 +160,9 @@
 
     row_max, row_sum, row_pos = carry
     row_lse = row_max + jnp.log(row_sum)
-    first = lax.broadcasted_iota(jnp.int32, (8, users), 0) == 0
-    stats = jnp.where(first, row_lse, row_pos)
+    rows = users // 128
+    stats = jnp.concatenate([part[:, 128 * k:128 * (k + 1)] for part in (row_lse, row_pos)
+                             for k in range(rows)], axis=0)
     row_send[...] = stats
     for d in range(1, n_item):
         to_item(row_send, row_recv.at[i], row_ssem.at[d], row_rsem.at[i], item_at(d)).start()
@@ -163,10 +171,10 @@
     for d in range(1, n_item):
         q = item_at(d)
         to_item(row_send, row_recv.at[q], row_ssem.at[0], row_rsem.at[q], i).wait_recv()
-    lse_all = row_recv[:, 0, :]
-    top = jnp.max(lse_all, axis=0, keepdims=True)
-    total = top + jnp.log(jnp.sum(jnp.exp(lse_all - top), axis=0, keepdims=True))
-    row_ref[...] = total - jnp.sum(row_recv[:, 1, :], axis=0, keepdims=True)
+    lse_all = row_recv[:, 0:rows, :]
+    top = jnp.max(lse_all, axis=0)
+    total = top + jnp.log(jnp.sum(jnp.exp(lse_all - top), axis=0))
+    row_ref[...] = total - jnp.sum(row_recv[:, rows:2 * rows, :], axis=0)
 
     for d in range(1, n_user):
         p = user_at(d)
@@ -194,28 +202,31 @@
     per, d_in = item_features.shape
     d_hid, d_emb = layer_two.shape
     users = user_vectors.shape[0]
-    anywhere = pl.BlockSpec(memory_space=pl.ANY)
+    anywhere = pl.BlockSpec(memory_space=pltpu.HBM)
     vmem = pl.BlockSpec(memory_space=pltpu.VMEM)
     dma = pltpu.SemaphoreType.DMA
     row, col = pl.pallas_call(
         functools.partial(kernel, n_user, n_item, n_y),
-        out_shape=(jax.ShapeDtypeStruct((1, users), jnp.float32),
+        out_shape=(jax.ShapeDtypeStruct((users // 128, 128), jnp.float32),
                    jax.ShapeDtypeStruct((1, per), jnp.float32)),
-        in_specs=[anywhere, anywhere, anywhere, vmem, anywhere, vmem],
+        in_specs=[anywhere] * 6,
         out_specs=(vmem, vmem),
         scratch_shapes=[
             pltpu.VMEM((per, d_in), jnp.bfloat16),
             pltpu.VMEM((d_in, d_hid), jnp.bfloat16),
             pltpu.VMEM((d_hid, d_emb), jnp.bfloat16),
             pltpu.VMEM((users, d_emb), jnp.bfloat16),
+            pltpu.VMEM((d_emb, users), jnp.bfloat16),
+            pltpu.VMEM((1, per), jnp.float32),
+            pltpu.VMEM((1, users), jnp.int32),
             pltpu.VMEM((per, d_hid), jnp.bfloat16),
             pltpu.VMEM((n_user, per, d_emb), jnp.bfloat16),
             pltpu.VMEM((n_user, 8, 128), jnp.float32),
             pltpu.VMEM((n_user, 8, 128), jnp.float32),
             pltpu.VMEM((n_user, 8, 128), jnp.float32),
-            pltpu.VMEM((8, users), jnp.float32),
-            pltpu.VMEM((n_item, 8, users), jnp.float32),
-            dma((3,)),
+            pltpu.VMEM((users // 64, 128), jnp.float32),
+            pltpu.VMEM((n_item, users // 64, 128), jnp.float32),
+            dma((5,)),
             dma((CHUNKS,)),
             dma((n_user,)),
             dma((n_user,)),
@@ -228,7 +239,7 @@
             dma((n_item,)),
         ],
         compiler_params=pltpu.CompilerParams(
-            collective_id=0, has_side_effects=True, vmem_limit_bytes=40 * 1024 * 1024),
+            collective_id=0, has_side_effects=True, vmem_limit_bytes=62 * 1024 * 1024),
     )(item_features, layer_one, layer_two, log_weight.reshape(1, per), user_vectors,
       positive_index.reshape(1, users))
     return row.reshape(users), col.reshape(per)

time: 33.5 us -> 28.4 us (0.85)
  local copies, waits for them, and re-layouts: 7.82 us -> 2.39 us
  Pallas kernels: 24.7 us -> 25.2 us
    unnamed x14 -> x2, local copies, waits for them, and re-layouts: 7.82 us -> 2.39 us
    pallas_call x1, Pallas kernels: 24.7 us -> 25.2 us  [on_device(): pl.pallas_call(functools.partial(kernel, n_user, n_item, n_y), out_shape=...]
where the time goes in v2:
time: 28.4 us; the launch traced here: 28.3 us
  Pallas kernels  25.2 us (89%)
  local copies, waits for them, and re-layouts  2.39 us (8%)
  between operations  0.64 us (2%)
    pallas_call x1, Pallas kernels, on_device(): pl.pallas_call(functools.partial(kernel, n_user, n_item, n_y), out_shape=...  25.2 us
    unnamed x2, local copies, waits for them, and re-layouts  2.39 us

profile of v2, /device:TPU:0, one launch (start us, length us, event | category | flops | bytes accessed | tf_op | source)
XLA Modules:
  0.0 28.3 jit_solution(3021493172670409440)
XLA Ops:
  0.6 25.2 %shard_map.77 = (f32[4,128]{1,0:T(4,128)}, f32[1,64]{1,0:T(1,128)}) custom-call(bf16[64,2048]{1,0:T(8,128)(2,1)} %x_hbm.1, bf16[2048,1024]{1,0:T(8,128)(2,1)} %w1_hbm.1, bf16[1024,512]{1,0:T(8,128)(2,1)} %w2_hbm.1, f32[1,64]{1,0:T(1,128)} %bitcast.6, bf16[512,512]{1,0:T(8,128)(2,1)} %uv_hbm.1, s32[1,512]{1,0:T(1,128)} %bitcast.4), custom_call_target="tpu_custom_call" | custom-call | tf_op jit(solution)/shard_map/pallas_call | solution.py:208
  25.9 1.2 %copy.10 = f32[512]{0:T(512)} copy(f32[512]{0:T(512)} %bitcast.5) | data formatting | bytes 4096
  27.1 1.1 %copy.11 = f32[64]{0:T(128)} copy(f32[64]{0:T(128)} %bitcast.7) | data formatting | bytes 512

commit v3 on v2

v3 whole, which is shorter than its diff:
```python
import functools
import math

import jax
import jax.numpy as jnp
from jax import lax
from jax.experimental import pallas as pl
from jax.experimental.pallas import tpu as pltpu
from jax.sharding import PartitionSpec as P

MESH = pl.DeviceIdType.MESH
CHUNKS = 4
PARTS = 2


def kernel(n_user, n_item, n_y, x_hbm, w1_hbm, w2_hbm, lw_hbm, uv_hbm, pos_hbm, row_ref, col_ref,
           xv, w1v, w2v, uvb, uvt, posb, lwv, emb, lwg, col_part, col_send, col_recv, row_send, row_recv,
           in_sem, w1_sem, lw_ssem, lw_rsem, emb_ssem, emb_rsem, col_ssem, col_rsem,
           uv_ssem, uv_rsem, pos_ssem, pos_rsem, row_ssem, row_rsem):
    n_z = n_user // n_y
    u = lax.axis_index("user")
    i = lax.axis_index("item")
    z, y = u // n_y, u % n_y
    core = lax.rem(i, 2)
    mate = i + 1 - 2 * core
    per = xv.shape[0]
    users = uvb.shape[1]
    half = users // 2
    sub = half // PARTS
    rows = users // 128
    inverse_temp = 4.0 / math.sqrt(uvb.shape[2])
    deep = w1v.shape[0] // CHUNKS

    cx = pltpu.make_async_copy(x_hbm, xv, in_sem.at[0])
    cx.start()
    c1 = []
    for c in range(CHUNKS):
        part = pl.ds(c * deep, deep)
        c1.append(pltpu.make_async_copy(w1_hbm.at[part], w1v.at[part], w1_sem.at[c]))
        c1[-1].start()
    c2 = pltpu.make_async_copy(w2_hbm, w2v, in_sem.at[1])
    c2.start()
    cu = pltpu.make_async_copy(uv_hbm, uvb.at[0], in_sem.at[2])
    cu.start()
    cp = pltpu.make_async_copy(pos_hbm, posb.at[0], in_sem.at[3])
    cp.start()
    cw = pltpu.make_async_copy(lw_hbm, lwv, in_sem.at[4])
    cw.start()

    def z_to(d):
        return {"user": lax.rem(z + d, n_z) * n_y + y}

    def y_to(e):
        return {"user": z * n_y + lax.rem(y + e, n_y)}

    def plane_to(k, e):
        return {"user": z * n_y + lax.rem(y + e, n_y), "item": lax.rem(i + k, n_item)}

    plane = [(k, e) for e in range(n_y - 1, -1, -1) for k in range(n_item) if (k, e) != (0, 0)]

    barrier = pltpu.get_barrier_semaphore()
    for d in range(1, n_z):
        pl.semaphore_signal(barrier, inc=1, device_id=z_to(d), device_id_type=MESH)
    for k, e in plane:
        pl.semaphore_signal(barrier, inc=1, device_id=plane_to(k, e), device_id_type=MESH)

    def remote(src, dst, ssem, rsem, to):
        return pltpu.make_async_remote_copy(src_ref=src, dst_ref=dst, send_sem=ssem, recv_sem=rsem,
                                            device_id=to, device_id_type=MESH)

    def lw_copy(d):
        return remote(lwg.at[0], lwg.at[d], lw_ssem.at[d], lw_rsem.at[d], z_to(d))

    def emb_copy(d):
        return remote(emb.at[0], emb.at[d], emb_ssem.at[d], emb_rsem.at[d], z_to(d))

    def col_copy(d):
        return remote(col_send.at[d], col_recv.at[d], col_ssem.at[d], col_rsem.at[d], z_to(n_z - d))

    def uv_copy(e, s):
        part = pl.ds(pl.multiple_of(core * half + s * sub, sub), sub)
        return remote(uv_hbm.at[part], uvb.at[e, part], uv_ssem.at[e, 0, s], uv_rsem.at[e, 0, s], y_to(e))

    def uv_share(e, s):
        part = pl.ds(pl.multiple_of(core * half + s * sub, sub), sub)
        return remote(uvb.at[e, part], uvb.at[e, part], uv_ssem.at[e, 1, s], uv_rsem.at[e, 1, s],
                      {"item": mate})

    def pos_copy(e):
        return remote(pos_hbm, posb.at[e], pos_ssem.at[e], pos_rsem.at[e], y_to(e))

    def row_copy(k, e):
        return remote(row_send.at[e], row_recv.at[k, e], row_ssem.at[k, e], row_rsem.at[k, e],
                      plane_to(k, e))

    lwg[0] = jnp.zeros((8, 128), jnp.float32)
    cw.wait()
    lwg[0, 0:1, 0:per] = lwv[...]

    cx.wait()
    hidden = None
    for c in range(CHUNKS):
        c1[c].wait()
        part = jnp.dot(xv[:, c * deep:(c + 1) * deep], w1v[c * deep:(c + 1) * deep, :],
                       preferred_element_type=jnp.float32)
        hidden = part if c == 0 else hidden + part
        if c == 0:
            pl.semaphore_wait(barrier, n_z - 1 + len(plane))
            for s in range(PARTS):
                for e in range(1, n_y):
                    uv_copy(e, s).start()
            for e in range(1, n_y):
                pos_copy(e).start()
            for d in range(1, n_z):
                lw_copy(d).start()
    hidden = jnp.maximum(hidden, 0.0).astype(jnp.bfloat16)
    c2.wait()
    emb[0] = jnp.dot(hidden, w2v[...], preferred_element_type=jnp.float32).astype(jnp.bfloat16)
    for d in range(1, n_z):
        emb_copy(d).start()

    eye = (lax.broadcasted_iota(jnp.int32, (per, 128), 0)
           == lax.broadcasted_iota(jnp.int32, (per, 128), 1))
    item_of = lax.broadcasted_iota(jnp.int32, (per, users), 0)

    def turn(e):
        for r in range(0, users, 128):
            uvt[e, :, r:r + 128] = uvb[e, r:r + 128, :].T

    def block(d, e, carry):
        row_max, row_sum, row_pos = carry
        scores = jnp.dot(emb[d], uvt[e], preferred_element_type=jnp.float32) * inverse_temp
        top = jnp.max(scores, axis=1, keepdims=True)
        lse = top + jnp.log(jnp.sum(jnp.exp(scores - top), axis=1, keepdims=True))
        col_part[d, e:e + 1, :] = jnp.sum(jnp.where(eye, lse, 0.0), axis=0, keepdims=True)
        weight = jnp.sum(jnp.where(eye, lwg[d, 0:1, :], 0.0), axis=1, keepdims=True)
        logits = scores + weight
        new_max = jnp.maximum(row_max, jnp.max(logits, axis=0, keepdims=True))
        row_sum = row_sum * jnp.exp(row_max - new_max) + jnp.sum(
            jnp.exp(logits - new_max), axis=0, keepdims=True)
        start = (i * n_user + lax.rem(z + n_z - d, n_z) * n_y + y) * per
        hits = posb[e] == start + item_of
        row_pos = row_pos + jnp.sum(jnp.where(hits, logits, 0.0), axis=0, keepdims=True)
        return new_max, row_sum, row_pos

    def joined(parts):
        top = jnp.max(parts, axis=0, keepdims=True)
        return top + jnp.log(jnp.sum(jnp.exp(parts - top), axis=0, keepdims=True))

    def col_stats(d):
        return jnp.broadcast_to(joined(col_part[d, 0:n_y, :]), (8, 128))

    def send_col(d):
        col_send[d] = col_stats(d)
        col_copy(d).start()

    def loop(low, high, step, carry):
        if n_z <= 4:
            for d in range(low, high):
                carry = step(d, carry)
            return carry
        return lax.fori_loop(low, high, step, carry)

    empty = (jnp.full((1, users), -1e30, jnp.float32), jnp.zeros((1, users), jnp.float32),
             jnp.zeros((1, users), jnp.float32))

    cu.wait()
    cp.wait()
    turn(0)
    own = block(0, 0, empty)

    def own_step(d, carry):
        lw_copy(d).wait_recv()
        emb_copy(d).wait_recv()
        return block(d, 0, carry)

    last = n_z - 1
    for s in range(PARTS):
        for e in range(1, n_y):
            uv_copy(e, s).wait_recv()
            uv_share(e, s).start()
        if s == 0:
            own = loop(1, min(2, last), own_step, own)
    own = loop(min(2, last), last, own_step, own)

    others = []
    for e in range(1, n_y):
        pos_copy(e).wait_recv()
        for s in range(PARTS):
            uv_share(e, s).wait_recv()
        turn(e)
        others.append(loop(0, last, lambda d, carry, e=e: block(d, e, carry), empty))

    def send_step(d, carry):
        send_col(d)
        return carry

    loop(1, last, send_step, 0)
    if last > 0:
        own = own_step(last, own)
        others = [block(last, e, others[e - 1]) for e in range(1, n_y)]
        send_col(last)
    col_recv[0] = col_stats(0)

    for e, carry in enumerate([own] + others):
        row_max, row_sum, row_pos = carry
        row_lse = row_max + jnp.log(row_sum)
        row_send[(n_y - e) % n_y] = jnp.concatenate(
            [part[:, 128 * k:128 * (k + 1)] for part in (row_lse, row_pos) for k in range(rows)], axis=0)
    for k, e in plane:
        row_copy(k, e).start()
    row_recv[0, 0] = row_send[0]

    for d in range(1, n_z):
        col_copy(d).wait_recv()
    col_ref[...] = joined(col_recv[:, 0, :])[:, 0:per]

    for k, e in plane:
        row_copy(k, e).wait_recv()
    stats = row_recv[...].reshape(n_item * n_y, 2 * rows, 128)
    lse_all = stats[:, 0:rows, :]
    top = jnp.max(lse_all, axis=0)
    total = top + jnp.log(jnp.sum(jnp.exp(lse_all - top), axis=0))
    row_ref[...] = total - jnp.sum(stats[:, rows:2 * rows, :], axis=0)

    for d in range(1, n_z):
        lw_copy(d).wait_send()
        emb_copy(d).wait_send()
        col_copy(d).wait_send()
    for e in range(1, n_y):
        pos_copy(e).wait_send()
        for s in range(PARTS):
            uv_copy(e, s).wait_send()
            uv_share(e, s).wait_send()
    for k, e in plane:
        row_copy(k, e).wait_send()


def hand_out(row_in, col_in, row_out, col_out, sem):
    first = pltpu.make_async_copy(row_in, row_out, sem.at[0])
    second = pltpu.make_async_copy(col_in, col_out, sem.at[1])
    first.start()
    second.start()
    first.wait()
    second.wait()


def on_device(n_user, n_item, n_y, item_features, layer_one, layer_two, log_weight, user_vectors,
              positive_index):
    per, d_in = item_features.shape
    d_hid, d_emb = layer_two.shape
    users = user_vectors.shape[0]
    n_z = n_user // n_y
    rows = users // 128
    anywhere = pl.BlockSpec(memory_space=pltpu.HBM)
    vmem = pl.BlockSpec(memory_space=pltpu.VMEM)
    dma = pltpu.SemaphoreType.DMA
    shapes = (jax.ShapeDtypeStruct((rows, 128), jnp.float32),
              jax.ShapeDtypeStruct((1, per), jnp.float32))
    row, col = pl.pallas_call(
        functools.partial(kernel, n_user, n_item, n_y),
        out_shape=shapes,
        in_specs=[anywhere] * 6,
        out_specs=(vmem, vmem),
        scratch_shapes=[
            pltpu.VMEM((per, d_in), jnp.bfloat16),
            pltpu.VMEM((d_in, d_hid), jnp.bfloat16),
            pltpu.VMEM((d_hid, d_emb), jnp.bfloat16),
            pltpu.VMEM((n_y, users, d_emb), jnp.bfloat16),
            pltpu.VMEM((n_y, d_emb, users), jnp.bfloat16),
            pltpu.VMEM((n_y, 1, users), jnp.int32),
            pltpu.VMEM((1, per), jnp.float32),
            pltpu.VMEM((n_z, per, d_emb), jnp.bfloat16),
            pltpu.VMEM((n_z, 8, 128), jnp.float32),
            pltpu.VMEM((n_z, 8, 128), jnp.float32),
            pltpu.VMEM((n_z, 8, 128), jnp.float32),
            pltpu.VMEM((n_z, 8, 128), jnp.float32),
            pltpu.VMEM((n_y, 2 * rows, 128), jnp.float32),
            pltpu.VMEM((n_item, n_y, 2 * rows, 128), jnp.float32),
            dma((5,)),
            dma((CHUNKS,)),
            dma((n_z,)),
            dma((n_z,)),
            dma((n_z,)),
            dma((n_z,)),
            dma((n_z,)),
            dma((n_z,)),
            dma((n_y, 2, PARTS)),
            dma((n_y, 2, PARTS)),
            dma((n_y,)),
            dma((n_y,)),
            dma((n_item, n_y)),
            dma((n_item, n_y)),
        ],
        compiler_params=pltpu.CompilerParams(
            collective_id=0, has_side_effects=True, vmem_limit_bytes=62 * 1024 * 1024),
    )(item_features, layer_one, layer_two, log_weight.reshape(1, per), user_vectors,
      positive_index.reshape(1, users))
    row, col = pl.pallas_call(
        hand_out,
        out_shape=shapes,
        in_specs=[anywhere] * 2,
        out_specs=(anywhere, anywhere),
        scratch_shapes=[dma((2,))],
        compiler_params=pltpu.CompilerParams(vmem_limit_bytes=62 * 1024 * 1024),
    )(row, col)
    return row.reshape(users), col.reshape(per)


def solution(mesh):
    n_user, n_item = mesh.shape["user"], mesh.shape["item"]
    n_y = 1
    while n_user % (2 * n_y) == 0 and 8 * n_y * n_y <= n_user:
        n_y *= 2
    placed = (P(("item", "user"), None), P(), P(), P(("item", "user")), P("user", None), P("user"))
    return jax.shard_map(
        functools.partial(on_device, n_user, n_item, n_y),
        mesh=mesh,
        in_specs=placed,
        out_specs=(P("user"), P(("item", "user"))),
        check_vma=False,
    )
```

time: 28.4 us -> 22.6 us (0.80)
  Pallas kernels: 25.2 us -> 21.8 us
  local copies, waits for them, and re-layouts: 2.39 us -> 0 us
    pallas_call x1, Pallas kernels: 25.2 us -> 20.6 us  [on_device(): pl.pallas_call(functools.partial(kernel, n_user, n_item, n_y), out_shape=...]
    unnamed x2 -> x0, local copies, waits for them, and re-layouts: 2.39 us -> none
    pallas_call x0 -> x1, Pallas kernels: none -> 1.2 us  [on_device(): pl.pallas_call(hand_out, out_shape=shapes, in_specs=[anywhere] * 2, out_s...]
where the time goes in v3:
time: 22.6 us; the launch traced here: 22.5 us
  Pallas kernels  21.8 us (96%)
  between operations  0.64 us (3%)
    pallas_call x1, Pallas kernels, on_device(): pl.pallas_call(functools.partial(kernel, n_user, n_item, n_y), out_shape=...  20.6 us
    pallas_call x1, Pallas kernels, on_device(): pl.pallas_call(hand_out, out_shape=shapes, in_specs=[anywhere] * 2, out_s...  1.2 us

profile of v3, /device:TPU:0, one launch (start us, length us, event | category | flops | bytes accessed | tf_op | source)
XLA Modules:
  0.0 22.5 jit_solution(3944420522981464091)
XLA Ops:
  0.6 20.6 %shard_map.77 = (f32[4,128]{1,0:T(4,128)}, f32[1,64]{1,0:T(1,128)}) custom-call(bf16[64,2048]{1,0:T(8,128)(2,1)} %x_hbm.1, bf16[2048,1024]{1,0:T(8,128)(2,1)} %w1_hbm.1, bf16[1024,512]{1,0:T(8,128)(2,1)} %w2_hbm.1, f32[1,64]{1,0:T(1,128)} %bitcast.5, bf16[512,512]{1,0:T(8,128)(2,1)} %uv_hbm.1, s32[1,512]{1,0:T(1,128)} %bitcast.4), custom_call_target="tpu_custom_call" | custom-call | tf_op jit(solution)/shard_map/pallas_call | solution.py:260
  21.3 1.2 %shard_map.78 = (f32[4,128]{1,0:T(4,128)}, f32[1,64]{1,0:T(1,128)}) custom-call(f32[4,128]{1,0:T(4,128)} %get-tuple-element.6.row_in, f32[1,64]{1,0:T(1,128)} %get-tuple-element.7.col_in), custom_call_target="tpu_custom_call" | custom-call | tf_op jit(solution)/shard_map/pallas_call | solution.py:299

commit v4 on v3

--- a/solution.py
+++ b/solution.py
@@ -24,15 +24,19 @@
     core = lax.rem(i, 2)
     mate = i + 1 - 2 * core
     per = xv.shape[0]
-    users = uvb.shape[1]
+    users, d_emb = uvb.shape
     half = users // 2
-    sub = half // PARTS
+    sub = d_emb // PARTS
     rows = users // 128
-    inverse_temp = 4.0 / math.sqrt(uvb.shape[2])
+    inverse_temp = 4.0 / math.sqrt(d_emb)
     deep = w1v.shape[0] // CHUNKS
 
+    cu = pltpu.make_async_copy(uv_hbm, uvb, in_sem.at[2])
+    cu.start()
     cx = pltpu.make_async_copy(x_hbm, xv, in_sem.at[0])
     cx.start()
+    cw = pltpu.make_async_copy(lw_hbm, lwv, in_sem.at[4])
+    cw.start()
     c1 = []
     for c in range(CHUNKS):
         part = pl.ds(c * deep, deep)
@@ -40,12 +44,8 @@
         c1[-1].start()
     c2 = pltpu.make_async_copy(w2_hbm, w2v, in_sem.at[1])
     c2.start()
-    cu = pltpu.make_async_copy(uv_hbm, uvb.at[0], in_sem.at[2])
-    cu.start()
     cp = pltpu.make_async_copy(pos_hbm, posb.at[0], in_sem.at[3])
     cp.start()
-    cw = pltpu.make_async_copy(lw_hbm, lwv, in_sem.at[4])
-    cw.start()
 
     def z_to(d):
         return {"user": lax.rem(z + d, n_z) * n_y + y}
@@ -78,13 +78,14 @@
         return remote(col_send.at[d], col_recv.at[d], col_ssem.at[d], col_rsem.at[d], z_to(n_z - d))
 
     def uv_copy(e, s):
-        part = pl.ds(pl.multiple_of(core * half + s * sub, sub), sub)
-        return remote(uv_hbm.at[part], uvb.at[e, part], uv_ssem.at[e, 0, s], uv_rsem.at[e, 0, s], y_to(e))
+        part = pl.ds(s * sub, sub)
+        return remote(uvt.at[0, core, part], uvt.at[e, core, part],
+                      uv_ssem.at[e, 0, s], uv_rsem.at[e, 0, s], y_to(e))
 
     def uv_share(e, s):
-        part = pl.ds(pl.multiple_of(core * half + s * sub, sub), sub)
-        return remote(uvb.at[e, part], uvb.at[e, part], uv_ssem.at[e, 1, s], uv_rsem.at[e, 1, s],
-                      {"item": mate})
+        part = pl.ds(s * sub, sub)
+        return remote(uvt.at[e, core, part], uvt.at[e, core, part],
+                      uv_ssem.at[e, 1, s], uv_rsem.at[e, 1, s], {"item": mate})
 
     def pos_copy(e):
         return remote(pos_hbm, posb.at[e], pos_ssem.at[e], pos_rsem.at[e], y_to(e))
@@ -96,6 +97,21 @@
     lwg[0] = jnp.zeros((8, 128), jnp.float32)
     cw.wait()
     lwg[0, 0:1, 0:per] = lwv[...]
+
+    def turn(h):
+        uvt[0, h] = uvb[pl.ds(pl.multiple_of(h * half, half), half), :].T
+
+    cu.wait()
+    turn(core)
+    pl.semaphore_wait(barrier, n_z - 1 + len(plane))
+    for s in range(PARTS):
+        for e in range(1, n_y):
+            uv_copy(e, s).start()
+    for d in range(1, n_z):
+        lw_copy(d).start()
+    for e in range(1, n_y):
+        pos_copy(e).start()
+    turn(1 - core)
 
     cx.wait()
     hidden = None
@@ -104,15 +120,6 @@
         part = jnp.dot(xv[:, c * deep:(c + 1) * deep], w1v[c * deep:(c + 1) * deep, :],
                        preferred_element_type=jnp.float32)
         hidden = part if c == 0 else hidden + part
-        if c == 0:
-            pl.semaphore_wait(barrier, n_z - 1 + len(plane))
-            for s in range(PARTS):
-                for e in range(1, n_y):
-                    uv_copy(e, s).start()
-            for e in range(1, n_y):
-                pos_copy(e).start()
-            for d in range(1, n_z):
-                lw_copy(d).start()
     hidden = jnp.maximum(hidden, 0.0).astype(jnp.bfloat16)
     c2.wait()
     emb[0] = jnp.dot(hidden, w2v[...], preferred_element_type=jnp.float32).astype(jnp.bfloat16)
@@ -121,25 +128,22 @@
 
     eye = (lax.broadcasted_iota(jnp.int32, (per, 128), 0)
            == lax.broadcasted_iota(jnp.int32, (per, 128), 1))
-    item_of = lax.broadcasted_iota(jnp.int32, (per, users), 0)
-
-    def turn(e):
-        for r in range(0, users, 128):
-            uvt[e, :, r:r + 128] = uvb[e, r:r + 128, :].T
-
-    def block(d, e, carry):
+    item_of = lax.broadcasted_iota(jnp.int32, (per, half), 0)
+
+    def block(d, e, slot, h, carry):
         row_max, row_sum, row_pos = carry
-        scores = jnp.dot(emb[d], uvt[e], preferred_element_type=jnp.float32) * inverse_temp
+        scores = jnp.dot(emb[d], uvt[e, h], preferred_element_type=jnp.float32) * inverse_temp
         top = jnp.max(scores, axis=1, keepdims=True)
         lse = top + jnp.log(jnp.sum(jnp.exp(scores - top), axis=1, keepdims=True))
-        col_part[d, e:e + 1, :] = jnp.sum(jnp.where(eye, lse, 0.0), axis=0, keepdims=True)
+        row = 2 * e + slot
+        col_part[d, row:row + 1, :] = jnp.sum(jnp.where(eye, lse, 0.0), axis=0, keepdims=True)
         weight = jnp.sum(jnp.where(eye, lwg[d, 0:1, :], 0.0), axis=1, keepdims=True)
         logits = scores + weight
         new_max = jnp.maximum(row_max, jnp.max(logits, axis=0, keepdims=True))
         row_sum = row_sum * jnp.exp(row_max - new_max) + jnp.sum(
             jnp.exp(logits - new_max), axis=0, keepdims=True)
         start = (i * n_user + lax.rem(z + n_z - d, n_z) * n_y + y) * per
-        hits = posb[e] == start + item_of
+        hits = posb[e, h] == start + item_of
         row_pos = row_pos + jnp.sum(jnp.where(hits, logits, 0.0), axis=0, keepdims=True)
         return new_max, row_sum, row_pos
 
@@ -148,7 +152,7 @@
         return top + jnp.log(jnp.sum(jnp.exp(parts - top), axis=0, keepdims=True))
 
     def col_stats(d):
-        return jnp.broadcast_to(joined(col_part[d, 0:n_y, :]), (8, 128))
+        return jnp.broadcast_to(joined(col_part[d, 0:2 * n_y, :]), (8, 128))
 
     def send_col(d):
         col_send[d] = col_stats(d)
@@ -161,35 +165,40 @@
             return carry
         return lax.fori_loop(low, high, step, carry)
 
-    empty = (jnp.full((1, users), -1e30, jnp.float32), jnp.zeros((1, users), jnp.float32),
-             jnp.zeros((1, users), jnp.float32))
-
-    cu.wait()
-    cp.wait()
-    turn(0)
-    own = block(0, 0, empty)
+    empty = (jnp.full((1, half), -1e30, jnp.float32), jnp.zeros((1, half), jnp.float32),
+             jnp.zeros((1, half), jnp.float32))
+
+    def own_block(d, carry):
+        return tuple(block(d, 0, h, h, carry[h]) for h in range(2))
 
     def own_step(d, carry):
         lw_copy(d).wait_recv()
         emb_copy(d).wait_recv()
-        return block(d, 0, carry)
-
+        return own_block(d, carry)
+
+    halves = (core, 1 - core)
     last = n_z - 1
+    cp.wait()
+    own = own_block(0, (empty, empty))
     for s in range(PARTS):
         for e in range(1, n_y):
             uv_copy(e, s).wait_recv()
             uv_share(e, s).start()
         if s == 0:
             own = loop(1, min(2, last), own_step, own)
+    others = []
+    for e in range(1, n_y):
+        pos_copy(e).wait_recv()
+        others.append([loop(0, min(2, last), lambda d, carry, e=e: block(d, e, 0, halves[0], carry), empty)])
     own = loop(min(2, last), last, own_step, own)
-
-    others = []
-    for e in range(1, n_y):
-        pos_copy(e).wait_recv()
+    for e in range(1, n_y):
         for s in range(PARTS):
             uv_share(e, s).wait_recv()
-        turn(e)
-        others.append(loop(0, last, lambda d, carry, e=e: block(d, e, carry), empty))
+    for e in range(1, n_y):
+        first = others[e - 1][0]
+        others[e - 1] = [
+            loop(min(2, last), last, lambda d, carry, e=e: block(d, e, 0, halves[0], carry), first),
+            loop(0, last, lambda d, carry, e=e: block(d, e, 1, halves[1], carry), empty)]
 
     def send_step(d, carry):
         send_col(d)
@@ -198,15 +207,20 @@
     loop(1, last, send_step, 0)
     if last > 0:
         own = own_step(last, own)
-        others = [block(last, e, others[e - 1]) for e in range(1, n_y)]
+        others = [[block(last, e, k, halves[k], others[e - 1][k]) for k in range(2)]
+                  for e in range(1, n_y)]
         send_col(last)
     col_recv[0] = col_stats(0)
 
     for e, carry in enumerate([own] + others):
-        row_max, row_sum, row_pos = carry
-        row_lse = row_max + jnp.log(row_sum)
+        stats = [(row_max + jnp.log(row_sum), row_pos) for row_max, row_sum, row_pos in carry]
+        if e > 0:
+            low = [jnp.where(core == 0, a, b) for a, b in zip(*stats)]
+            high = [jnp.where(core == 0, b, a) for a, b in zip(*stats)]
+            stats = [low, high]
         row_send[(n_y - e) % n_y] = jnp.concatenate(
-            [part[:, 128 * k:128 * (k + 1)] for part in (row_lse, row_pos) for k in range(rows)], axis=0)
+            [stats[h][m][:, 128 * k:128 * (k + 1)] for m in range(2) for h in range(2)
+             for k in range(rows // 2)], axis=0)
     for k, e in plane:
         row_copy(k, e).start()
     row_recv[0, 0] = row_send[0]
@@ -266,9 +280,9 @@
             pltpu.VMEM((per, d_in), jnp.bfloat16),
             pltpu.VMEM((d_in, d_hid), jnp.bfloat16),
             pltpu.VMEM((d_hid, d_emb), jnp.bfloat16),
-            pltpu.VMEM((n_y, users, d_emb), jnp.bfloat16),
-            pltpu.VMEM((n_y, d_emb, users), jnp.bfloat16),
-            pltpu.VMEM((n_y, 1, users), jnp.int32),
+            pltpu.VMEM((users, d_emb), jnp.bfloat16),
+            pltpu.VMEM((n_y, 2, d_emb, users // 2), jnp.bfloat16),
+            pltpu.VMEM((n_y, 2, 1, users // 2), jnp.int32),
             pltpu.VMEM((1, per), jnp.float32),
             pltpu.VMEM((n_z, per, d_emb), jnp.bfloat16),
             pltpu.VMEM((n_z, 8, 128), jnp.float32),
@@ -295,7 +309,7 @@
         compiler_params=pltpu.CompilerParams(
             collective_id=0, has_side_effects=True, vmem_limit_bytes=62 * 1024 * 1024),
     )(item_features, layer_one, layer_two, log_weight.reshape(1, per), user_vectors,
-      positive_index.reshape(1, users))
+      positive_index.reshape(2, 1, users // 2))
     row, col = pl.pallas_call(
         hand_out,
         out_shape=shapes,

time: 22.6 us -> 22.4 us (level)
  no operation moved by 1% of the time
where the time goes in v4:
time: 22.4 us; the launch traced here: 22.3 us
  Pallas kernels  21.6 us (96%)
  between operations  0.64 us (3%)
    pallas_call x1, Pallas kernels, on_device(): pl.pallas_call(functools.partial(kernel, n_user, n_item, n_y), out_shape=...  20.4 us
    pallas_call x1, Pallas kernels, on_device(): pl.pallas_call(hand_out, out_shape=shapes, in_specs=[anywhere] * 2, out_s...  1.2 us

profile of v4, /device:TPU:0, one launch (start us, length us, event | category | flops | bytes accessed | tf_op | source)
XLA Modules:
  0.0 22.3 jit_solution(8388154676743221918)
XLA Ops:
  0.6 20.4 %shard_map.77 = (f32[4,128]{1,0:T(4,128)}, f32[1,64]{1,0:T(1,128)}) custom-call(bf16[64,2048]{1,0:T(8,128)(2,1)} %x_hbm.1, bf16[2048,1024]{1,0:T(8,128)(2,1)} %w1_hbm.1, bf16[1024,512]{1,0:T(8,128)(2,1)} %w2_hbm.1, f32[1,64]{1,0:T(1,128)} %bitcast.5, bf16[512,512]{1,0:T(8,128)(2,1)} %uv_hbm.1, s32[2,1,256]{2,1,0:T(1,128)} %bitcast.4), custom_call_target="tpu_custom_call" | custom-call | tf_op jit(solution)/shard_map/pallas_call | solution.py:274
  21.1 1.2 %shard_map.78 = (f32[4,128]{1,0:T(4,128)}, f32[1,64]{1,0:T(1,128)}) custom-call(f32[4,128]{1,0:T(4,128)} %get-tuple-element.6.row_in, f32[1,64]{1,0:T(1,128)} %get-tuple-element.7.col_in), custom_call_target="tpu_custom_call" | custom-call | tf_op jit(solution)/shard_map/pallas_call | solution.py:313

commit v5 on v4

--- a/solution.py
+++ b/solution.py
@@ -111,7 +111,6 @@
         lw_copy(d).start()
     for e in range(1, n_y):
         pos_copy(e).start()
-    turn(1 - core)
 
     cx.wait()
     hidden = None
@@ -125,6 +124,7 @@
     emb[0] = jnp.dot(hidden, w2v[...], preferred_element_type=jnp.float32).astype(jnp.bfloat16)
     for d in range(1, n_z):
         emb_copy(d).start()
+    turn(1 - core)
 
     eye = (lax.broadcasted_iota(jnp.int32, (per, 128), 0)
            == lax.broadcasted_iota(jnp.int32, (per, 128), 1))
@@ -273,7 +273,7 @@
               jax.ShapeDtypeStruct((1, per), jnp.float32))
     row, col = pl.pallas_call(
         functools.partial(kernel, n_user, n_item, n_y),
-        out_shape=shapes,
+        out_shape=(pltpu.VMEM((rows, 128), jnp.float32), pltpu.VMEM((1, per), jnp.float32)),
         in_specs=[anywhere] * 6,
         out_specs=(vmem, vmem),
         scratch_shapes=[
@@ -313,10 +313,10 @@
     row, col = pl.pallas_call(
         hand_out,
         out_shape=shapes,
-        in_specs=[anywhere] * 2,
+        in_specs=[pl.BlockSpec(memory_space=pl.ANY)] * 2,
         out_specs=(anywhere, anywhere),
         scratch_shapes=[dma((2,))],
-        compiler_params=pltpu.CompilerParams(vmem_limit_bytes=62 * 1024 * 1024),
+        compiler_params=pltpu.CompilerParams(vmem_limit_bytes=4 * 1024 * 1024),
     )(row, col)
     return row.reshape(users), col.reshape(per)
 

time: 22.4 us -> 21.1 us (0.942)
  Pallas kernels: 21.6 us -> 20.3 us
    pallas_call x1, Pallas kernels: 20.4 us -> 19.7 us  [on_device(): pl.pallas_call(functools.partial(kernel, n_user, n_item, n_y), out_shape=...]
    pallas_call x1, Pallas kernels: 1.2 us -> 0.6 us  [on_device(): pl.pallas_call(hand_out, out_shape=shapes, in_specs=[pl.BlockSpec(memory_...]
where the time goes in v5:
time: 21.1 us; the launch traced here: 21 us
  Pallas kernels  20.3 us (96%)
  between operations  0.64 us (3%)
    pallas_call x1, Pallas kernels, on_device(): pl.pallas_call(functools.partial(kernel, n_user, n_item, n_y), out_shape=...  19.7 us
    pallas_call x1, Pallas kernels, on_device(): pl.pallas_call(hand_out, out_shape=shapes, in_specs=[pl.BlockSpec(memory_...  0.6 us

profile of v5, /device:TPU:0, one launch (start us, length us, event | category | flops | bytes accessed | tf_op | source)
XLA Modules:
  0.0 21.0 jit_solution(6577565647361234765)
XLA Ops:
  0.6 19.7 %shard_map.77 = (f32[4,128]{1,0:T(4,128)S(1)}, f32[1,64]{1,0:T(1,128)S(1)}) custom-call(bf16[64,2048]{1,0:T(8,128)(2,1)} %x_hbm.1, bf16[2048,1024]{1,0:T(8,128)(2,1)} %w1_hbm.1, bf16[1024,512]{1,0:T(8,128)(2,1)} %w2_hbm.1, f32[1,64]{1,0:T(1,128)} %bitcast.5, bf16[512,512]{1,0:T(8,128)(2,1)} %uv_hbm.1, s32[2,1,256]{2,1,0:T(1,128)} %bitcast.4), custom_call_target="tpu_custom_call" | custom-call | tf_op jit(solution)/shard_map/pallas_call | solution.py:274
  20.4 0.6 %shard_map.78 = (f32[4,128]{1,0:T(4,128)}, f32[1,64]{1,0:T(1,128)}) custom-call(f32[4,128]{1,0:T(4,128)S(1)} %get-tuple-element.6.row_in, f32[1,64]{1,0:T(1,128)S(1)} %get-tuple-element.7.col_in), custom_call_target="tpu_custom_call" | custom-call | tf_op jit(solution)/shard_map/pallas_call | solution.py:313

commit v6 on v5

--- a/solution.py
+++ b/solution.py
@@ -47,6 +47,22 @@
     cp = pltpu.make_async_copy(pos_hbm, posb.at[0], in_sem.at[3])
     cp.start()
 
+    def other(k):
+        place = 0
+        for a in range(n_z):
+            near = sorted((b for b in range(n_z) if b != a),
+                          key=lambda b: (abs(b - a), abs(2 * b - n_z + 1)))
+            here = 1 - ((z - a) * (z - a) + n_z * n_z - 1) // (n_z * n_z)
+            place = place + near[k - 1] * here
+        return place
+
+    ordered = n_z <= 4
+    ahead = [0] + [lax.rem(other(k) - z + n_z, n_z) if ordered else k for k in range(1, n_z)]
+    behind = [0] + [lax.rem(z - other(k) + n_z, n_z) if ordered else k for k in range(1, n_z)]
+
+    def slot(k):
+        return behind[k] if ordered else k
+
     def z_to(d):
         return {"user": lax.rem(z + d, n_z) * n_y + y}
 
@@ -122,20 +138,20 @@
     hidden = jnp.maximum(hidden, 0.0).astype(jnp.bfloat16)
     c2.wait()
     emb[0] = jnp.dot(hidden, w2v[...], preferred_element_type=jnp.float32).astype(jnp.bfloat16)
-    for d in range(1, n_z):
-        emb_copy(d).start()
+    for k in range(1, n_z):
+        emb_copy(ahead[k]).start()
     turn(1 - core)
 
     eye = (lax.broadcasted_iota(jnp.int32, (per, 128), 0)
            == lax.broadcasted_iota(jnp.int32, (per, 128), 1))
     item_of = lax.broadcasted_iota(jnp.int32, (per, half), 0)
 
-    def block(d, e, slot, h, carry):
+    def block(d, e, side, h, carry):
         row_max, row_sum, row_pos = carry
         scores = jnp.dot(emb[d], uvt[e, h], preferred_element_type=jnp.float32) * inverse_temp
         top = jnp.max(scores, axis=1, keepdims=True)
         lse = top + jnp.log(jnp.sum(jnp.exp(scores - top), axis=1, keepdims=True))
-        row = 2 * e + slot
+        row = 2 * e + side
         col_part[d, row:row + 1, :] = jnp.sum(jnp.where(eye, lse, 0.0), axis=0, keepdims=True)
         weight = jnp.sum(jnp.where(eye, lwg[d, 0:1, :], 0.0), axis=1, keepdims=True)
         logits = scores + weight
@@ -171,7 +187,8 @@
     def own_block(d, carry):
         return tuple(block(d, 0, h, h, carry[h]) for h in range(2))
 
-    def own_step(d, carry):
+    def own_step(k, carry):
+        d = slot(k)
         lw_copy(d).wait_recv()
         emb_copy(d).wait_recv()
         return own_block(d, carry)
@@ -189,7 +206,7 @@
     others = []
     for e in range(1, n_y):
         pos_copy(e).wait_recv()
-        others.append([loop(0, min(2, last), lambda d, carry, e=e: block(d, e, 0, halves[0], carry), empty)])
+        others.append([loop(0, min(2, last), lambda k, carry, e=e: block(slot(k), e, 0, halves[0], carry), empty)])
     own = loop(min(2, last), last, own_step, own)
     for e in range(1, n_y):
         for s in range(PARTS):
@@ -197,19 +214,19 @@
     for e in range(1, n_y):
         first = others[e - 1][0]
         others[e - 1] = [
-            loop(min(2, last), last, lambda d, carry, e=e: block(d, e, 0, halves[0], carry), first),
-            loop(0, last, lambda d, carry, e=e: block(d, e, 1, halves[1], carry), empty)]
-
-    def send_step(d, carry):
-        send_col(d)
+            loop(min(2, last), last, lambda k, carry, e=e: block(slot(k), e, 0, halves[0], carry), first),
+            loop(0, last, lambda k, carry, e=e: block(slot(k), e, 1, halves[1], carry), empty)]
+
+    def send_step(k, carry):
+        send_col(slot(k))
         return carry
 
     loop(1, last, send_step, 0)
     if last > 0:
         own = own_step(last, own)
-        others = [[block(last, e, k, halves[k], others[e - 1][k]) for k in range(2)]
+        others = [[block(slot(last), e, k, halves[k], others[e - 1][k]) for k in range(2)]
                   for e in range(1, n_y)]
-        send_col(last)
+        send_col(slot(last))
     col_recv[0] = col_stats(0)
 
     for e, carry in enumerate([own] + others):

time: 21.1 us -> 21.5 us (1.019)
  Pallas kernels: 20.3 us -> 20.7 us
    pallas_call x1, Pallas kernels: 19.7 us -> 20.1 us  [on_device(): pl.pallas_call(functools.partial(kernel, n_user, n_item, n_y), out_shape=...]
where the time goes in v6:
time: 21.5 us; the launch traced here: 21.3 us
  Pallas kernels  20.7 us (96%)
  between operations  0.64 us (3%)
    pallas_call x1, Pallas kernels, on_device(): pl.pallas_call(functools.partial(kernel, n_user, n_item, n_y), out_shape=...  20.1 us
    pallas_call x1, Pallas kernels, on_device(): pl.pallas_call(hand_out, out_shape=shapes, in_specs=[pl.BlockSpec(memory_...  0.6 us

profile of v6, /device:TPU:0, one launch (start us, length us, event | category | flops | bytes accessed | tf_op | source)
XLA Modules:
  0.0 21.3 jit_solution(1445489336108233960)
XLA Ops:
  0.6 20.1 %shard_map.77 = (f32[4,128]{1,0:T(4,128)S(1)}, f32[1,64]{1,0:T(1,128)S(1)}) custom-call(bf16[64,2048]{1,0:T(8,128)(2,1)} %x_hbm.1, bf16[2048,1024]{1,0:T(8,128)(2,1)} %w1_hbm.1, bf16[1024,512]{1,0:T(8,128)(2,1)} %w2_hbm.1, f32[1,64]{1,0:T(1,128)} %bitcast.5, bf16[512,512]{1,0:T(8,128)(2,1)} %uv_hbm.1, s32[2,1,256]{2,1,0:T(1,128)} %bitcast.4), custom_call_target="tpu_custom_call" | custom-call | tf_op jit(solution)/shard_map/pallas_call | solution.py:291
  20.7 0.6 %shard_map.78 = (f32[4,128]{1,0:T(4,128)}, f32[1,64]{1,0:T(1,128)}) custom-call(f32[4,128]{1,0:T(4,128)S(1)} %get-tuple-element.6.row_in, f32[1,64]{1,0:T(1,128)S(1)} %get-tuple-element.7.col_in), custom_call_target="tpu_custom_call" | custom-call | tf_op jit(solution)/shard_map/pallas_call | solution.py:330

commit v7 on v5

--- a/solution.py
+++ b/solution.py
@@ -130,9 +130,11 @@
            == lax.broadcasted_iota(jnp.int32, (per, 128), 1))
     item_of = lax.broadcasted_iota(jnp.int32, (per, half), 0)
 
-    def block(d, e, slot, h, carry):
+    def block(d, e, slot, h, carry, scores=None):
         row_max, row_sum, row_pos = carry
-        scores = jnp.dot(emb[d], uvt[e, h], preferred_element_type=jnp.float32) * inverse_temp
+        if scores is None:
+            scores = jnp.dot(emb[d], uvt[e, h], preferred_element_type=jnp.float32)
+        scores = scores * inverse_temp
         top = jnp.max(scores, axis=1, keepdims=True)
         lse = top + jnp.log(jnp.sum(jnp.exp(scores - top), axis=1, keepdims=True))
         row = 2 * e + slot
@@ -177,39 +179,44 @@
         return own_block(d, carry)
 
     halves = (core, 1 - core)
-    last = n_z - 1
     cp.wait()
     own = own_block(0, (empty, empty))
     for s in range(PARTS):
         for e in range(1, n_y):
             uv_copy(e, s).wait_recv()
             uv_share(e, s).start()
-        if s == 0:
-            own = loop(1, min(2, last), own_step, own)
+    early = min(2, n_z)
+    for d in range(1, early):
+        own = own_step(d, own)
+    for e in range(1, n_y):
+        pos_copy(e).wait_recv()
+        for s in range(PARTS):
+            uv_share(e, s).wait_recv()
+
+    rows_here = emb[0:early].reshape(early * per, d_emb)
     others = []
     for e in range(1, n_y):
-        pos_copy(e).wait_recv()
-        others.append([loop(0, min(2, last), lambda d, carry, e=e: block(d, e, 0, halves[0], carry), empty)])
-    own = loop(min(2, last), last, own_step, own)
-    for e in range(1, n_y):
-        for s in range(PARTS):
-            uv_share(e, s).wait_recv()
-    for e in range(1, n_y):
-        first = others[e - 1][0]
-        others[e - 1] = [
-            loop(min(2, last), last, lambda d, carry, e=e: block(d, e, 0, halves[0], carry), first),
-            loop(0, last, lambda d, carry, e=e: block(d, e, 1, halves[1], carry), empty)]
-
-    def send_step(d, carry):
+        pair = []
+        for k in range(2):
+            scores = jnp.dot(rows_here, uvt[e, halves[k]], preferred_element_type=jnp.float32)
+            carry = empty
+            for d in range(early):
+                carry = block(d, e, k, halves[k], carry, scores[d * per:(d + 1) * per])
+            pair.append(carry)
+        others.append(tuple(pair))
+    for d in range(1, early):
         send_col(d)
-        return carry
-
-    loop(1, last, send_step, 0)
-    if last > 0:
-        own = own_step(last, own)
-        others = [[block(last, e, k, halves[k], others[e - 1][k]) for k in range(2)]
-                  for e in range(1, n_y)]
-        send_col(last)
+
+    def full_step(d, carry):
+        own, others = carry
+        own = own_step(d, own)
+        others = tuple(tuple(block(d, e, k, halves[k], others[e - 1][k]) for k in range(2))
+                       for e in range(1, n_y))
+        send_col(d)
+        return own, others
+
+    own, others = loop(early, n_z, full_step, (own, tuple(others)))
+    others = list(others)
     col_recv[0] = col_stats(0)
 
     for e, carry in enumerate([own] + others):

time: 21.1 us -> 20.6 us (0.976)
  Pallas kernels: 20.3 us -> 19.8 us
    pallas_call x1, Pallas kernels: 19.7 us -> 19.2 us  [on_device(): pl.pallas_call(functools.partial(kernel, n_user, n_item, n_y), out_shape=...]
where the time goes in v7:
time: 20.6 us; the launch traced here: 20.5 us
  Pallas kernels  19.8 us (96%)
  between operations  0.64 us (3%)
    pallas_call x1, Pallas kernels, on_device(): pl.pallas_call(functools.partial(kernel, n_user, n_item, n_y), out_shape=...  19.2 us
    pallas_call x1, Pallas kernels, on_device(): pl.pallas_call(hand_out, out_shape=shapes, in_specs=[pl.BlockSpec(memory_...  0.6 us

profile of v7, /device:TPU:0, one launch (start us, length us, event | category | flops | bytes accessed | tf_op | source)
XLA Modules:
  0.0 20.5 jit_solution(10555010049150552464)
XLA Ops:
  0.6 19.2 %shard_map.77 = (f32[4,128]{1,0:T(4,128)S(1)}, f32[1,64]{1,0:T(1,128)S(1)}) custom-call(bf16[64,2048]{1,0:T(8,128)(2,1)} %x_hbm.1, bf16[2048,1024]{1,0:T(8,128)(2,1)} %w1_hbm.1, bf16[1024,512]{1,0:T(8,128)(2,1)} %w2_hbm.1, f32[1,64]{1,0:T(1,128)} %bitcast.5, bf16[512,512]{1,0:T(8,128)(2,1)} %uv_hbm.1, s32[2,1,256]{2,1,0:T(1,128)} %bitcast.4), custom_call_target="tpu_custom_call" | custom-call | tf_op jit(solution)/shard_map/pallas_call | solution.py:281
  19.9 0.6 %shard_map.78 = (f32[4,128]{1,0:T(4,128)}, f32[1,64]{1,0:T(1,128)}) custom-call(f32[4,128]{1,0:T(4,128)S(1)} %get-tuple-element.6.row_in, f32[1,64]{1,0:T(1,128)S(1)} %get-tuple-element.7.col_in), custom_call_target="tpu_custom_call" | custom-call | tf_op jit(solution)/shard_map/pallas_call | solution.py:320

commit v8 on v7

--- a/solution.py
+++ b/solution.py
@@ -185,7 +185,7 @@
         for e in range(1, n_y):
             uv_copy(e, s).wait_recv()
             uv_share(e, s).start()
-    early = min(2, n_z)
+    early = 2 if n_z % 2 == 0 else 1
     for d in range(1, early):
         own = own_step(d, own)
     for e in range(1, n_y):
@@ -207,15 +207,28 @@
     for d in range(1, early):
         send_col(d)
 
-    def full_step(d, carry):
+    def full_step(j, carry):
         own, others = carry
-        own = own_step(d, own)
-        others = tuple(tuple(block(d, e, k, halves[k], others[e - 1][k]) for k in range(2))
+        group = [j * early + k for k in range(early)]
+        for d in group:
+            lw_copy(d).wait_recv()
+            emb_copy(d).wait_recv()
+        rows_now = emb[pl.ds(j * early, early)].reshape(early * per, d_emb)
+
+        def meet(e, slot, h, carry):
+            scores = jnp.dot(rows_now, uvt[e, h], preferred_element_type=jnp.float32)
+            for k, d in enumerate(group):
+                carry = block(d, e, slot, h, carry, scores[k * per:(k + 1) * per])
+            return carry
+
+        others = tuple(tuple(meet(e, k, halves[k], others[e - 1][k]) for k in range(2))
                        for e in range(1, n_y))
-        send_col(d)
+        own = tuple(meet(0, h, h, own[h]) for h in range(2))
+        for d in group:
+            send_col(d)
         return own, others
 
-    own, others = loop(early, n_z, full_step, (own, tuple(others)))
+    own, others = loop(1, n_z // early, full_step, (own, tuple(others)))
     others = list(others)
     col_recv[0] = col_stats(0)
 

time: 20.6 us -> 20.2 us (0.981)
  Pallas kernels: 19.8 us -> 19.4 us
    pallas_call x1, Pallas kernels: 19.2 us -> 18.8 us  [on_device(): pl.pallas_call(functools.partial(kernel, n_user, n_item, n_y), out_shape=...]
where the time goes in v8:
time: 20.2 us; the launch traced here: 20 us
  Pallas kernels  19.4 us (96%)
  between operations  0.64 us (3%)
    pallas_call x1, Pallas kernels, on_device(): pl.pallas_call(functools.partial(kernel, n_user, n_item, n_y), out_shape=...  18.8 us
    pallas_call x1, Pallas kernels, on_device(): pl.pallas_call(hand_out, out_shape=shapes, in_specs=[pl.BlockSpec(memory_...  0.6 us

profile of v8, /device:TPU:0, one launch (start us, length us, event | category | flops | bytes accessed | tf_op | source)
XLA Modules:
  0.0 20.0 jit_solution(3180709604407757896)
XLA Ops:
  0.6 18.8 %shard_map.77 = (f32[4,128]{1,0:T(4,128)S(1)}, f32[1,64]{1,0:T(1,128)S(1)}) custom-call(bf16[64,2048]{1,0:T(8,128)(2,1)} %x_hbm.1, bf16[2048,1024]{1,0:T(8,128)(2,1)} %w1_hbm.1, bf16[1024,512]{1,0:T(8,128)(2,1)} %w2_hbm.1, f32[1,64]{1,0:T(1,128)} %bitcast.5, bf16[512,512]{1,0:T(8,128)(2,1)} %uv_hbm.1, s32[2,1,256]{2,1,0:T(1,128)} %bitcast.4), custom_call_target="tpu_custom_call" | custom-call | tf_op jit(solution)/shard_map/pallas_call | solution.py:294
  19.4 0.6 %shard_map.78 = (f32[4,128]{1,0:T(4,128)}, f32[1,64]{1,0:T(1,128)}) custom-call(f32[4,128]{1,0:T(4,128)S(1)} %get-tuple-element.6.row_in, f32[1,64]{1,0:T(1,128)S(1)} %get-tuple-element.7.col_in), custom_call_target="tpu_custom_call" | custom-call | tf_op jit(solution)/shard_map/pallas_call | solution.py:333

commit v9 on v8

--- a/solution.py
+++ b/solution.py
@@ -32,7 +32,6 @@
     deep = w1v.shape[0] // CHUNKS
 
     cu = pltpu.make_async_copy(uv_hbm, uvb, in_sem.at[2])
-    cu.start()
     cx = pltpu.make_async_copy(x_hbm, xv, in_sem.at[0])
     cx.start()
     cw = pltpu.make_async_copy(lw_hbm, lwv, in_sem.at[4])
@@ -42,6 +41,8 @@
         part = pl.ds(c * deep, deep)
         c1.append(pltpu.make_async_copy(w1_hbm.at[part], w1v.at[part], w1_sem.at[c]))
         c1[-1].start()
+        if c == 0:
+            cu.start()
     c2 = pltpu.make_async_copy(w2_hbm, w2v, in_sem.at[1])
     c2.start()
     cp = pltpu.make_async_copy(pos_hbm, posb.at[0], in_sem.at[3])
@@ -100,17 +101,6 @@
 
     def turn(h):
         uvt[0, h] = uvb[pl.ds(pl.multiple_of(h * half, half), half), :].T
-
-    cu.wait()
-    turn(core)
-    pl.semaphore_wait(barrier, n_z - 1 + len(plane))
-    for s in range(PARTS):
-        for e in range(1, n_y):
-            uv_copy(e, s).start()
-    for d in range(1, n_z):
-        lw_copy(d).start()
-    for e in range(1, n_y):
-        pos_copy(e).start()
 
     cx.wait()
     hidden = None
@@ -119,6 +109,17 @@
         part = jnp.dot(xv[:, c * deep:(c + 1) * deep], w1v[c * deep:(c + 1) * deep, :],
                        preferred_element_type=jnp.float32)
         hidden = part if c == 0 else hidden + part
+        if c == 0:
+            cu.wait()
+            turn(core)
+            pl.semaphore_wait(barrier, n_z - 1 + len(plane))
+            for s in range(PARTS):
+                for e in range(1, n_y):
+                    uv_copy(e, s).start()
+            for d in range(1, n_z):
+                lw_copy(d).start()
+            for e in range(1, n_y):
+                pos_copy(e).start()
     hidden = jnp.maximum(hidden, 0.0).astype(jnp.bfloat16)
     c2.wait()
     emb[0] = jnp.dot(hidden, w2v[...], preferred_element_type=jnp.float32).astype(jnp.bfloat16)

time: 20.2 us -> 20.1 us (level)
  no operation moved by 1% of the time
where the time goes in v9:
time: 20.1 us; the launch traced here: 19.9 us
  Pallas kernels  19.3 us (96%)
  between operations  0.64 us (3%)
    pallas_call x1, Pallas kernels, on_device(): pl.pallas_call(functools.partial(kernel, n_user, n_item, n_y), out_shape=...  18.7 us
    pallas_call x1, Pallas kernels, on_device(): pl.pallas_call(hand_out, out_shape=shapes, in_specs=[pl.BlockSpec(memory_...  0.6 us

profile of v9, /device:TPU:0, one launch (start us, length us, event | category | flops | bytes accessed | tf_op | source)
XLA Modules:
  0.0 19.9 jit_solution(1412163070910586566)
XLA Ops:
  0.6 18.7 %shard_map.77 = (f32[4,128]{1,0:T(4,128)S(1)}, f32[1,64]{1,0:T(1,128)S(1)}) custom-call(bf16[64,2048]{1,0:T(8,128)(2,1)} %x_hbm.1, bf16[2048,1024]{1,0:T(8,128)(2,1)} %w1_hbm.1, bf16[1024,512]{1,0:T(8,128)(2,1)} %w2_hbm.1, f32[1,64]{1,0:T(1,128)} %bitcast.5, bf16[512,512]{1,0:T(8,128)(2,1)} %uv_hbm.1, s32[2,1,256]{2,1,0:T(1,128)} %bitcast.4), custom_call_target="tpu_custom_call" | custom-call | tf_op jit(solution)/shard_map/pallas_call | solution.py:295
  19.3 0.6 %shard_map.78 = (f32[4,128]{1,0:T(4,128)}, f32[1,64]{1,0:T(1,128)}) custom-call(f32[4,128]{1,0:T(4,128)S(1)} %get-tuple-element.6.row_in, f32[1,64]{1,0:T(1,128)S(1)} %get-tuple-element.7.col_in), custom_call_target="tpu_custom_call" | custom-call | tf_op jit(solution)/shard_map/pallas_call | solution.py:334
